TPU v7x, 256 devices: a whole 4x4x8 slice. The times are simulated.
256 devices in a mesh: tm: 4 (over x), pair: 64 (over z, y, core).
Axes of the slice: x: 4, y: 4, z: 8, core: 2. Of those that a mesh axis runs over, the one named last changes fastest.
Arguments:
- strain: bfloat16 [8, 8192, 8192], P('tm', 'pair'), may hold values from -80 to 80
- pair_list: int32 [4096, 2], replicated, may hold values from 0 to 4095, as said below
- pair_bins: int32 [4096], P('pair'), may hold values from 0 to 511, as said below
- bin_slots: int32 [512], replicated, may hold values from 0 to 511, as said below
- seg_valid: int32 [8], P('tm'), may hold values 0 or 1
Outputs:
- stacked: float32 [512, 2048], P('pair', 'tm')
Inputs may be any that keep to these rules, and one draw needn't show every extreme that they name: `pair_list`: the 64 rows of one index of pair name, over both columns, exactly 2 different blocks of every device, block g lying on index g // 64; the two blocks of a pair differ. `pair_bins`: bin n belongs to index bin_slots[n] // 8 of pair. The rows of one index of pair name at most 3 pairs whose bins belong to one index; 8 indices receive exactly 3 from every index. `bin_slots`: A permutation of the stack's rows.
All inputs are finite; a program needn't handle non-finite values. No bound on the sum of `seg_valid` on one device may be relied on, other than what follows from the above.
Results may differ from a plain program's by a relative error of at most 0.011.
Values may be sent and summed in bfloat16 or wider, within the bound.
A program may use at most 128 MiB of HBM per device.

v0:
```python
import functools
import math

import jax
import jax.numpy as jnp
import numpy as np
from jax import lax
from jax.experimental import pallas as pl
from jax.experimental.pallas import tpu as pltpu
from jax.sharding import PartitionSpec as P

SEG_LEN = 8192
BAND = 1024
FIRST_BIN = 128
LAGS = 2048
EPS = 1e-06
NPAIR = 64
NTM = 4
SUB = SEG_LEN // 8
MESH = pl.DeviceIdType.MESH
F32 = jnp.float32
BF16 = jnp.bfloat16


def owned_bins():
    bins = np.zeros((4, 16, 2, 8), np.int64)
    for c in range(4):
        for a in range(2):
            k1 = (0, 4)[a] if c == 0 else (c, 8 - c)[a]
            for w in range(16):
                bins[c, w, a] = k1 + 8 * (16 + 8 * w + np.arange(8))
    return bins


def forward_tables():
    bins = owned_bins()
    t = np.arange(SUB, dtype=np.int64)
    theta = (bins[..., None] * t % SEG_LEN) * (2.0 * math.pi / SEG_LEN)
    cos, sin = np.cos(theta), np.sin(theta)
    table = np.zeros((4, 16, 2, 2, 8, 2, SUB), np.float64)
    sign = (1.0, -1.0)
    for c in range(4):
        for a in range(2):
            if c == 0:
                table[c, :, 0, a, :, a] = cos[c, :, a]
                table[c, :, 1, a, :, a] = -sin[c, :, a]
            else:
                table[c, :, 0, a, :, 0] = cos[c, :, a]
                table[c, :, 0, a, :, 1] = sign[a] * sin[c, :, a]
                table[c, :, 1, a, :, 0] = -sin[c, :, a]
                table[c, :, 1, a, :, 1] = sign[a] * cos[c, :, a]
    return table.reshape(4, 512, 2 * SUB).astype(jnp.bfloat16)


def inverse_tables():
    bins = owned_bins().reshape(NPAIR, 16)
    lag = np.arange(LAGS, dtype=np.int64) - LAGS // 2
    phi = (bins[..., None] * lag % SEG_LEN) * (2.0 * math.pi / SEG_LEN)
    factor = 1.0 / math.sqrt(BAND)
    table = np.stack([np.cos(phi) * factor, -np.sin(phi) * factor], axis=1)
    table = table.reshape(2 * BAND, NTM, LAGS // NTM).transpose(1, 0, 2)
    return np.ascontiguousarray(table).astype(jnp.bfloat16)


def fold_table():
    table = np.zeros((4, 2, 2, 2, 2, 16, 4, 2, 16), np.float32)
    for q in range(4):
        for b in range(16):
            table[q, 0, 0, :, :, b, q, 0, b] = 1.0
            table[q, 0, 1, :, :, b, q, 0, b] = 1.0
            table[q, 1, 0, :, :, b, q, 1, b] = -1.0
            table[q, 1, 1, :, :, b, q, 1, b] = 1.0
    return table.reshape(1024, 128).astype(jnp.bfloat16)


def iota(shape, dim):
    return lax.broadcasted_iota(jnp.int32, shape, dim)


def dot(a, b):
    return jnp.dot(a, b, preferred_element_type=F32)


def dot_nt(a, b):
    return lax.dot_general(a, b, (((1,), (1,)), ((), ())), preferred_element_type=F32)


def body(
    x_hbm, tab_hbm, inv_hbm, fold_ref, pairs_ref, bins_smem, slots_smem, valid_smem,
    out_ref,
    x_buf, tab_buf, inv_buf, y_buf, r_buf, send_buf, recv_buf, id_buf,
    src_rows, loc_rows, loc_mat, g1_buf, g2_buf, s_buf, rows_buf, p_buf,
    part_buf, got_buf, spec_buf,
    load_sem, send_sem, recv_sem, id_send, id_recv, part_send, part_recv, x_send, x_recv,
):
    tm = lax.axis_index("tm")
    me = lax.axis_index("pair")

    def x_load(s):
        return pltpu.make_async_copy(x_hbm.at[s], x_buf.at[s], load_sem.at[s])

    def tab_load(c):
        return pltpu.make_async_copy(tab_hbm.at[c], tab_buf.at[c], load_sem.at[2 + c])

    inv_load = pltpu.make_async_copy(inv_hbm.at[tm], inv_buf, load_sem.at[6])
    x_load(0).start()
    x_load(1).start()
    for c in range(4):
        tab_load(c).start()
    inv_load.start()

    barrier = pltpu.get_barrier_semaphore()

    def greet(i, _):
        pl.semaphore_signal(barrier, inc=1, device_id=(tm, lax.rem(me + i, NPAIR)), device_id_type=MESH)
        return 0

    lax.fori_loop(1, NPAIR, greet, 0)
    for i in range(1, NTM):
        pl.semaphore_signal(barrier, inc=1, device_id=(lax.rem(tm + i, NTM), me), device_id_type=MESH)

    lane = iota((1, 128), 1)
    first_lane = lax.rem(me, 2) * 64

    def one_id(k, row):
        r = slots_smem[bins_smem[k]]
        code = (r & 3) * 128 + (r >> 3) * 2 + ((r >> 2) & 1)
        return jnp.where(lane == first_lane + k, code, row)

    id_buf[me] = lax.fori_loop(0, 64, one_id, jnp.zeros((1, 128), jnp.int32))

    root = math.sqrt(0.5)
    for s in range(2):
        x_load(s).wait()

        def split(step, _):
            rows = pl.ds(pl.multiple_of(step * 16, 16), 16)
            to = pl.ds(pl.multiple_of(s * 128 + step * 16, 16), 16)
            for h in range(2):
                v = [
                    x_buf[s, rows, e * SUB + h * 512 : e * SUB + h * 512 + 512].astype(F32)
                    for e in range(8)
                ]
                s04, s26, s15, s37 = v[0] + v[4], v[2] + v[6], v[1] + v[5], v[3] + v[7]
                d04, d26, d15, d37 = v[0] - v[4], v[2] - v[6], v[1] - v[5], v[3] - v[7]
                even, odd = s04 + s26, s15 + s37
                diff, both = (d15 - d37) * root, (d15 + d37) * root
                parts = (
                    (even + odd, even - odd),
                    (d04 + diff, -d26 - both),
                    (s04 - s26, s37 - s15),
                    (d04 - diff, d26 - both),
                )
                for c in range(4):
                    for part in range(2):
                        at = part * SUB + h * 512
                        y_buf[c, to, at : at + 512] = parts[c][part].astype(BF16)
            return 0

        lax.fori_loop(0, 8, split, 0)

    for c in range(4):
        tab_load(c).wait()
        r_buf[c] = dot_nt(tab_buf[c], y_buf[c])

    def white(w, _):
        rows = pl.ds(pl.multiple_of(w * 32, 32), 32)
        parts = [r_buf[c, rows, :] for c in range(4)]
        power = parts[0] * parts[0]
        for c in range(1, 4):
            power = power + parts[c] * parts[c]
        energy = jnp.sum(power, axis=0, keepdims=True) * (1.0 / 64.0)
        scale = 1.0 / jnp.sqrt(energy + EPS)
        for c in range(4):
            done = (parts[c] * scale).astype(BF16)
            send_buf[c * 16 + w, 0:32, :] = done[:, 0:128]
            send_buf[c * 16 + w, 32:64, :] = done[:, 128:256]
        return 0

    lax.fori_loop(0, 16, white, 0)

    pl.semaphore_wait(barrier, NPAIR - 1 + NTM - 1)

    def id_copy(d):
        return pltpu.make_async_remote_copy(
            src_ref=id_buf.at[me], dst_ref=id_buf.at[me], send_sem=id_send.at[d],
            recv_sem=id_recv.at[me], device_id=(tm, d), device_id_type=MESH,
        )

    def main_copy(d):
        return pltpu.make_async_remote_copy(
            src_ref=send_buf.at[d], dst_ref=recv_buf.at[me], send_sem=send_sem.at[d],
            recv_sem=recv_sem.at[me], device_id=(tm, d), device_id_type=MESH,
        )

    def arrival(buf, sems, s):
        return pltpu.make_async_copy(buf.at[s], buf.at[s], sems.at[s])

    def send_all(i, _):
        d = lax.rem(me + i, NPAIR)
        id_copy(d).start()
        main_copy(d).start()
        return 0

    lax.fori_loop(1, NPAIR, send_all, 0)
    recv_buf[me] = send_buf[me]

    low = iota((1, 128), 1) < 64
    for q in range(32):
        a = pairs_ref[0:1, q * 128 : q * 128 + 128]
        b = pairs_ref[1:2, q * 128 : q * 128 + 128]
        first = jnp.where(low, a, pltpu.roll(b, 64, 1))
        second = jnp.where(low, pltpu.roll(a, 64, 1), b)
        for j, row in enumerate((first, second)):
            src_rows[2 * q + j : 2 * q + j + 1, :] = (row >> 6).astype(F32)
            loc_rows[2 * q + j : 2 * q + j + 1, :] = (row & 63).astype(F32)
    src_rows[64:128, :] = jnp.zeros((64, 128), F32)
    src_cols = src_rows[...].T.astype(BF16)
    lane_sq = iota((128, 128), 1)
    sub_sq = iota((128, 128), 0)
    lane_f = lane_sq.astype(F32)
    ones_sq = jnp.ones((128, 128), BF16)
    group = 8

    def ask(step, _):
        base = step * group
        pick = (iota((128, group * 128), 0) == base + iota((128, group * 128), 1) // 128)
        src_b = dot(src_cols, pick.astype(BF16))
        cols = [src_b[:, j * 128 : j * 128 + 128] for j in range(group)]
        earlier = []
        for j in range(group):
            row = src_rows[pl.ds(base + j, 1), :]
            hit = jnp.logical_and(cols[j] == row, lane_sq < sub_sq)
            earlier.append(jnp.where(hit, 1.0, 0.0).astype(BF16))
        slot_b = dot(jnp.concatenate(earlier, axis=0), ones_sq)
        for j in range(group):
            code = 2.0 * cols[j] + slot_b[j * 128 : j * 128 + 128]
            g2 = jnp.where(code == lane_f, 1.0, 0.0).astype(BF16)
            g2_buf[base + j] = g2
            loc = jnp.broadcast_to(loc_rows[pl.ds(base + j, 1), :], (16, 128)).astype(BF16)
            loc_mat[pl.ds(base + j, 1), :] = dot(loc, g2)[0:1, :]
        return 0

    lax.fori_loop(0, NPAIR // group, ask, 0)

    loc_cols = loc_mat[...].astype(BF16)

    def choose(s, _):
        pick = iota((128, 256), 0) == 2 * s + iota((128, 256), 1) // 128
        loc_b = dot(loc_cols, pick.astype(BF16))
        loc_b = 2.0 * jnp.concatenate([loc_b[:, 0:128], loc_b[:, 128:256]], axis=0)
        g1_buf[s, :, 0:128] = jnp.where(loc_b == lane_f, 1.0, 0.0).astype(BF16)
        g1_buf[s, :, 128:256] = jnp.where(loc_b + 1.0 == lane_f, 1.0, 0.0).astype(BF16)
        return 0

    lax.fori_loop(0, NPAIR, choose, 0, unroll=4)

    def id_wait(i, _):
        arrival(id_buf, id_recv, lax.rem(me + NPAIR - i, NPAIR)).wait()
        return 0

    lax.fori_loop(1, NPAIR, id_wait, 0)
    for q in range(32):
        row = id_buf[2 * q] + id_buf[2 * q + 1]
        hit = iota((512, 128), 0) == row
        s_buf[:, q * 128 : q * 128 + 128] = jnp.where(hit, 1.0, 0.0).astype(BF16)

    zero = jnp.zeros((16, 128), BF16)

    def take(i, _):
        s = lax.rem(me + NPAIR - i, NPAIR)

        @pl.when(i > 0)
        def _():
            arrival(recv_buf, recv_sem, s).wait()

        piece = [[recv_buf[s, (2 * g + ri) * 16 : (2 * g + ri) * 16 + 16, :] for ri in range(2)] for g in range(2)]
        rows = []
        for ri in range(2):
            for ch in range(2):
                for g in range(2):
                    halves = [piece[g][ri], zero] if ch == 0 else [zero, piece[g][ri]]
                    rows.append(jnp.concatenate(halves, axis=1))
        rows_buf[pl.ds(pl.multiple_of(s * 128, 128), 128), :] = dot_nt(
            g1_buf[s], jnp.concatenate(rows, axis=0)
        )
        return 0

    lax.fori_loop(0, NPAIR, take, 0)

    def cross(p, _):
        asked = rows_buf[pl.ds(p, 128, stride=64), :].astype(BF16)
        sides = dot(g2_buf[p], asked)
        left, right = sides[0:64], sides[64:128]
        to = pl.ds(pl.multiple_of(p * 64, 64), 64)
        p_buf[to, 0:128] = (left * right).astype(BF16)
        p_buf[to, 128:256] = (left * pltpu.roll(right, 64, 1)).astype(BF16)
        return 0

    lax.fori_loop(0, NPAIR, cross, 0, unroll=4)

    seg = (iota((1, 256), 1) >> 4) & 1
    weight = jnp.where(seg == 0, valid_smem[0], valid_smem[1]).astype(F32)
    total = jnp.zeros((128, 128), F32)
    for q in range(4):
        z = dot(s_buf[q * 128 : q * 128 + 128, :], p_buf[...]) * weight
        high = z.astype(BF16)
        rest = (z - high.astype(F32)).astype(BF16)
        fold = fold_ref[q * 256 : q * 256 + 256, :]
        total = total + (dot(high, fold) + dot(rest, fold))
    for d in range(NPAIR):
        part_buf[d] = total[2 * d : 2 * d + 2, :]

    def part_copy(d):
        return pltpu.make_async_remote_copy(
            src_ref=part_buf.at[d], dst_ref=got_buf.at[me], send_sem=part_send.at[d],
            recv_sem=part_recv.at[me], device_id=(tm, d), device_id_type=MESH,
        )

    def send_parts(i, _):
        part_copy(lax.rem(me + i, NPAIR)).start()
        return 0

    lax.fori_loop(1, NPAIR, send_parts, 0)
    got_buf[me] = part_buf[me]

    def part_wait(i, _):
        arrival(got_buf, part_recv, lax.rem(me + NPAIR - i, NPAIR)).wait()
        return 0

    lax.fori_loop(1, NPAIR, part_wait, 0)

    sub8, lane8 = iota((8, 128), 0), iota((8, 128), 1)
    for tile in range(16):
        made = jnp.zeros((8, 128), F32)
        for j in range(4):
            two = got_buf[4 * tile + j]
            both = jnp.where(
                sub8 < 4,
                jnp.broadcast_to(two[0:1, :], (8, 128)),
                jnp.broadcast_to(two[1:2, :], (8, 128)),
            )
            for q in range(4):
                turned = pltpu.roll(both, (32 * (j - q)) % 128, 1) if j != q else both
                here = jnp.logical_and(sub8 % 4 == q, lane8 // 32 == j)
                made = jnp.where(here, turned, made)
        spec_buf[tm, :, tile * 128 : tile * 128 + 128] = made

    def x_copy(i):
        to = lax.rem(tm + i, NTM)
        return pltpu.make_async_remote_copy(
            src_ref=spec_buf.at[tm], dst_ref=spec_buf.at[tm], send_sem=x_send.at[to],
            recv_sem=x_recv.at[tm], device_id=(to, me), device_id_type=MESH,
        )

    for i in range(1, NTM):
        x_copy(i).start()
    inv_load.wait()
    for i in range(1, NTM):
        arrival(spec_buf, x_recv, lax.rem(tm + NTM - i, NTM)).wait()
    spec = (spec_buf[0] + spec_buf[1]) + (spec_buf[2] + spec_buf[3])
    high = spec.astype(BF16)
    rest = (spec - high.astype(F32)).astype(BF16)
    lags = dot(jnp.concatenate([high, rest], axis=0), inv_buf[...])
    out_ref[...] = lags[0:8] + lags[8:16]

    def sent(i, _):
        d = lax.rem(me + i, NPAIR)
        id_copy(d).wait_send()
        main_copy(d).wait_send()
        part_copy(d).wait_send()
        return 0

    lax.fori_loop(1, NPAIR, sent, 0)
    for i in range(1, NTM):
        x_copy(i).wait_send()


def on_device(strain, pair_list, pair_bins, bin_slots, seg_valid):
    vmem = pl.BlockSpec(memory_space=pltpu.VMEM)
    smem = pl.BlockSpec(memory_space=pltpu.SMEM)
    hbm = pl.BlockSpec(memory_space=pl.ANY)
    dma = pltpu.SemaphoreType.DMA
    return pl.pallas_call(
        body,
        out_shape=jax.ShapeDtypeStruct((8, LAGS // NTM), F32),
        in_specs=[hbm, hbm, hbm, vmem, vmem, smem, smem, smem],
        out_specs=vmem,
        scratch_shapes=[
            pltpu.VMEM((2, 128, SEG_LEN), BF16),
            pltpu.VMEM((4, 512, 2 * SUB), BF16),
            pltpu.VMEM((2 * BAND, LAGS // NTM), BF16),
            pltpu.VMEM((4, 256, 2 * SUB), BF16),
            pltpu.VMEM((4, 512, 256), F32),
            pltpu.VMEM((NPAIR, 64, 128), BF16),
            pltpu.VMEM((NPAIR, 64, 128), BF16),
            pltpu.VMEM((NPAIR, 1, 128), jnp.int32),
            pltpu.VMEM((128, 128), F32),
            pltpu.VMEM((64, 128), F32),
            pltpu.VMEM((64, 128), F32),
            pltpu.VMEM((NPAIR, 128, 256), BF16),
            pltpu.VMEM((NPAIR, 128, 128), BF16),
            pltpu.VMEM((512, 4096), BF16),
            pltpu.VMEM((NPAIR * 128, 128), F32),
            pltpu.VMEM((4096, 256), BF16),
            pltpu.VMEM((NPAIR, 2, 128), F32),
            pltpu.VMEM((NPAIR, 2, 128), F32),
            pltpu.VMEM((NTM, 8, 2 * BAND), F32),
            dma((7,)), dma((NPAIR,)), dma((NPAIR,)), dma((NPAIR,)), dma((NPAIR,)),
            dma((NPAIR,)), dma((NPAIR,)), dma((NTM,)), dma((NTM,)),
        ],
        compiler_params=pltpu.CompilerParams(
            collective_id=0, has_side_effects=True, vmem_limit_bytes=60 << 20
        ),
    )(
        strain,
        jnp.asarray(forward_tables()),
        jnp.asarray(inverse_tables()),
        jnp.asarray(fold_table()),
        pair_list.T,
        pair_bins,
        bin_slots,
        seg_valid,
    )


def solution(mesh):
    return jax.shard_map(
        on_device,
        mesh=mesh,
        in_specs=(P("tm", "pair", None), P(), P("pair"), P(), P("tm")),
        out_specs=P("pair", "tm"),
        check_vma=False,
    )
```

profile of v0, /device:TPU:1, one launch (start us, length us, event | category | flops | bytes accessed | tf_op | source)
XLA Modules:
  0.0 82.2 jit_solution(1528622681135236244)
XLA Ops:
  0.0 80.9 %shard_map.82 = f32[8,512]{1,0:T(8,128)} custom-call(bf16[2,128,8192]{2,1,0:T(8,128)(2,1)} %x_hbm.1, bf16[4,512,2048]{2,1,0:T(8,128)(2,1)} %constant.6.clone.tab_hbm, bf16[4,2048,512]{2,1,0:T(8,128)(2,1)} %constant.7.clone.inv_hbm, bf16[1024,128]{1,0:T(8,128)(2,1)} %constant.8.clone.fold_ref, s32[2,4096]{1,0:T(2,128)} %bitcast.1, s32[64]{0:T(128)} %bins_smem.1, ...), custom_call_target="tpu_custom_call" | custom-call | tf_op jit(solution)/shard_map/pallas_call | solution.py:384
  80.9 1.3 %copy.10 = f32[8,512]{1,0:T(8,128)} copy(f32[8,512]{1,0:T(8,128)} %shard_map.82) | data formatting | bytes 32768
where the time goes:
time: 82.4 us; the launch traced here: 82.2 us
  Pallas kernels  80.9 us (98%)
  local copies, waits for them, and re-layouts  1.32 us (2%)
    pallas_call x1, Pallas kernels, on_device(): pl.pallas_call(body, out_shape=jax.ShapeDtypeStruct((8, LAGS // NTM), F32...  80.9 us

commit v1 on v0

--- a/solution.py
+++ b/solution.py
@@ -16,6 +16,7 @@
 EPS = 1e-06
 NPAIR = 64
 NTM = 4
+GROUP = 8
 SUB = SEG_LEN // 8
 MESH = pl.DeviceIdType.MESH
 F32 = jnp.float32
@@ -90,8 +91,8 @@
     out_ref,
     x_buf, tab_buf, inv_buf, y_buf, r_buf, send_buf, recv_buf, id_buf,
     src_rows, loc_rows, loc_mat, g1_buf, g2_buf, s_buf, rows_buf, p_buf,
-    part_buf, got_buf, spec_buf,
-    load_sem, send_sem, recv_sem, id_send, id_recv, part_send, part_recv, x_send, x_recv,
+    part_buf, mid_buf, got_buf, spec_buf,
+    load_sem, send_sem, recv_sem, id_sem, part_sem, x_sem,
 ):
     tm = lax.axis_index("tm")
     me = lax.axis_index("pair")
@@ -181,28 +182,40 @@
 
     pl.semaphore_wait(barrier, NPAIR - 1 + NTM - 1)
 
-    def id_copy(d):
+    here = me // GROUP * GROUP
+    mine = lax.rem(me, GROUP)
+
+    def beside(i):
+        return here + lax.rem(mine + i, GROUP)
+
+    def across(i):
+        return lax.rem(me + i * GROUP, NPAIR)
+
+    def remote(src, dst, sems, to):
         return pltpu.make_async_remote_copy(
-            src_ref=id_buf.at[me], dst_ref=id_buf.at[me], send_sem=id_send.at[d],
-            recv_sem=id_recv.at[me], device_id=(tm, d), device_id_type=MESH,
+            src_ref=src, dst_ref=dst, send_sem=sems[0], recv_sem=sems[1],
+            device_id=to, device_id_type=MESH,
         )
 
-    def main_copy(d):
-        return pltpu.make_async_remote_copy(
-            src_ref=send_buf.at[d], dst_ref=recv_buf.at[me], send_sem=send_sem.at[d],
-            recv_sem=recv_sem.at[me], device_id=(tm, d), device_id_type=MESH,
-        )
-
-    def arrival(buf, sems, s):
-        return pltpu.make_async_copy(buf.at[s], buf.at[s], sems.at[s])
-
-    def send_all(i, _):
+    def landed(ref, sem):
+        return pltpu.make_async_copy(ref, ref, sem)
+
+    def main_copy(i):
         d = lax.rem(me + i, NPAIR)
-        id_copy(d).start()
-        main_copy(d).start()
-        return 0
-
-    lax.fori_loop(1, NPAIR, send_all, 0)
+        return remote(send_buf.at[d], recv_buf.at[me], (send_sem, recv_sem.at[me]), (tm, d))
+
+    def send_main(i, _):
+        main_copy(i).start()
+        return 0
+
+    for i in range(1, GROUP):
+        remote(id_buf.at[me], id_buf.at[me], (id_sem.at[0], id_sem.at[1]), (tm, beside(i))).start()
+    lax.fori_loop(1, 32, send_main, 0)
+    landed(id_buf.at[pl.ds(0, GROUP - 1)], id_sem.at[1]).wait()
+    own_group = id_buf.at[pl.ds(here, GROUP)]
+    for i in range(1, GROUP):
+        remote(own_group, own_group, (id_sem.at[2], id_sem.at[3]), (tm, across(i))).start()
+    lax.fori_loop(32, NPAIR, send_main, 0)
     recv_buf[me] = send_buf[me]
 
     low = iota((1, 128), 1) < 64
@@ -220,20 +233,20 @@
     sub_sq = iota((128, 128), 0)
     lane_f = lane_sq.astype(F32)
     ones_sq = jnp.ones((128, 128), BF16)
-    group = 8
+    asks = 8
 
     def ask(step, _):
-        base = step * group
-        pick = (iota((128, group * 128), 0) == base + iota((128, group * 128), 1) // 128)
+        base = step * asks
+        pick = (iota((128, asks * 128), 0) == base + iota((128, asks * 128), 1) // 128)
         src_b = dot(src_cols, pick.astype(BF16))
-        cols = [src_b[:, j * 128 : j * 128 + 128] for j in range(group)]
+        cols = [src_b[:, j * 128 : j * 128 + 128] for j in range(asks)]
         earlier = []
-        for j in range(group):
+        for j in range(asks):
             row = src_rows[pl.ds(base + j, 1), :]
             hit = jnp.logical_and(cols[j] == row, lane_sq < sub_sq)
             earlier.append(jnp.where(hit, 1.0, 0.0).astype(BF16))
         slot_b = dot(jnp.concatenate(earlier, axis=0), ones_sq)
-        for j in range(group):
+        for j in range(asks):
             code = 2.0 * cols[j] + slot_b[j * 128 : j * 128 + 128]
             g2 = jnp.where(code == lane_f, 1.0, 0.0).astype(BF16)
             g2_buf[base + j] = g2
@@ -241,7 +254,7 @@
             loc_mat[pl.ds(base + j, 1), :] = dot(loc, g2)[0:1, :]
         return 0
 
-    lax.fori_loop(0, NPAIR // group, ask, 0)
+    lax.fori_loop(0, NPAIR // asks, ask, 0)
 
     loc_cols = loc_mat[...].astype(BF16)
 
@@ -255,11 +268,7 @@
 
     lax.fori_loop(0, NPAIR, choose, 0, unroll=4)
 
-    def id_wait(i, _):
-        arrival(id_buf, id_recv, lax.rem(me + NPAIR - i, NPAIR)).wait()
-        return 0
-
-    lax.fori_loop(1, NPAIR, id_wait, 0)
+    landed(id_buf.at[pl.ds(0, NPAIR - GROUP)], id_sem.at[3]).wait()
     for q in range(32):
         row = id_buf[2 * q] + id_buf[2 * q + 1]
         hit = iota((512, 128), 0) == row
@@ -267,26 +276,35 @@
 
     zero = jnp.zeros((16, 128), BF16)
 
-    def take(i, _):
-        s = lax.rem(me + NPAIR - i, NPAIR)
-
-        @pl.when(i > 0)
-        def _():
-            arrival(recv_buf, recv_sem, s).wait()
-
-        piece = [[recv_buf[s, (2 * g + ri) * 16 : (2 * g + ri) * 16 + 16, :] for ri in range(2)] for g in range(2)]
-        rows = []
-        for ri in range(2):
-            for ch in range(2):
-                for g in range(2):
-                    halves = [piece[g][ri], zero] if ch == 0 else [zero, piece[g][ri]]
-                    rows.append(jnp.concatenate(halves, axis=1))
-        rows_buf[pl.ds(pl.multiple_of(s * 128, 128), 128), :] = dot_nt(
-            g1_buf[s], jnp.concatenate(rows, axis=0)
-        )
-        return 0
-
-    lax.fori_loop(0, NPAIR, take, 0)
+    batch = 4
+
+    def take(step, _):
+        first = step * batch
+        sources = [lax.rem(me + NPAIR - first - j, NPAIR) for j in range(batch)]
+        for j, s in enumerate(sources):
+            if j == 0:
+
+                @pl.when(first > 0)
+                def _():
+                    landed(recv_buf.at[s], recv_sem.at[s]).wait()
+
+            else:
+                landed(recv_buf.at[s], recv_sem.at[s]).wait()
+        for s in sources:
+            rows = []
+            for ri in range(2):
+                for ch in range(2):
+                    for g in range(2):
+                        at = (2 * g + ri) * 16
+                        piece = recv_buf[s, at : at + 16, :]
+                        halves = [piece, zero] if ch == 0 else [zero, piece]
+                        rows.append(jnp.concatenate(halves, axis=1))
+            rows_buf[pl.ds(pl.multiple_of(s * 128, 128), 128), :] = dot_nt(
+                g1_buf[s], jnp.concatenate(rows, axis=0)
+            )
+        return 0
+
+    lax.fori_loop(0, NPAIR // batch, take, 0)
 
     def cross(p, _):
         asked = rows_buf[pl.ds(p, 128, stride=64), :].astype(BF16)
@@ -297,7 +315,7 @@
         p_buf[to, 128:256] = (left * pltpu.roll(right, 64, 1)).astype(BF16)
         return 0
 
-    lax.fori_loop(0, NPAIR, cross, 0, unroll=4)
+    lax.fori_loop(0, NPAIR, cross, 0, unroll=8)
 
     seg = (iota((1, 256), 1) >> 4) & 1
     weight = jnp.where(seg == 0, valid_smem[0], valid_smem[1]).astype(F32)
@@ -309,32 +327,26 @@
         fold = fold_ref[q * 256 : q * 256 + 256, :]
         total = total + (dot(high, fold) + dot(rest, fold))
     for d in range(NPAIR):
-        part_buf[d] = total[2 * d : 2 * d + 2, :]
-
-    def part_copy(d):
-        return pltpu.make_async_remote_copy(
-            src_ref=part_buf.at[d], dst_ref=got_buf.at[me], send_sem=part_send.at[d],
-            recv_sem=part_recv.at[me], device_id=(tm, d), device_id_type=MESH,
-        )
-
-    def send_parts(i, _):
-        part_copy(lax.rem(me + i, NPAIR)).start()
-        return 0
-
-    lax.fori_loop(1, NPAIR, send_parts, 0)
-    got_buf[me] = part_buf[me]
-
-    def part_wait(i, _):
-        arrival(got_buf, part_recv, lax.rem(me + NPAIR - i, NPAIR)).wait()
-        return 0
-
-    lax.fori_loop(1, NPAIR, part_wait, 0)
+        part_buf[d // GROUP, d % GROUP] = total[2 * d : 2 * d + 2, :]
+
+    group = me // GROUP
+    for i in range(1, GROUP):
+        to = across(i)
+        remote(part_buf.at[to // GROUP], mid_buf.at[group], (part_sem.at[0], part_sem.at[1]), (tm, to)).start()
+    mid_buf[group] = part_buf[group]
+    landed(mid_buf.at[pl.ds(0, GROUP - 1)], part_sem.at[1]).wait()
+    for i in range(1, GROUP):
+        to = beside(i)
+        remote(mid_buf.at[:, lax.rem(to, GROUP)], got_buf.at[:, mine], (part_sem.at[2], part_sem.at[3]), (tm, to)).start()
+    got_buf[:, pl.ds(mine, 1)] = mid_buf[:, pl.ds(mine, 1)]
+    landed(got_buf.at[:, pl.ds(0, GROUP - 1)], part_sem.at[3]).wait()
 
     sub8, lane8 = iota((8, 128), 0), iota((8, 128), 1)
-    for tile in range(16):
+    def spread(tile):
         made = jnp.zeros((8, 128), F32)
         for j in range(4):
-            two = got_buf[4 * tile + j]
+            d = 4 * tile + j
+            two = got_buf[d // GROUP, d % GROUP]
             both = jnp.where(
                 sub8 < 4,
                 jnp.broadcast_to(two[0:1, :], (8, 128)),
@@ -342,38 +354,33 @@
             )
             for q in range(4):
                 turned = pltpu.roll(both, (32 * (j - q)) % 128, 1) if j != q else both
-                here = jnp.logical_and(sub8 % 4 == q, lane8 // 32 == j)
-                made = jnp.where(here, turned, made)
-        spec_buf[tm, :, tile * 128 : tile * 128 + 128] = made
-
-    def x_copy(i):
-        to = lax.rem(tm + i, NTM)
-        return pltpu.make_async_remote_copy(
-            src_ref=spec_buf.at[tm], dst_ref=spec_buf.at[tm], send_sem=x_send.at[to],
-            recv_sem=x_recv.at[tm], device_id=(to, me), device_id_type=MESH,
-        )
-
+                fits = jnp.logical_and(sub8 % 4 == q, lane8 // 32 == j)
+                made = jnp.where(fits, turned, made)
+        return made
+
+    for tile in range(8):
+        both = jnp.concatenate([spread(tile), spread(tile + 8)], axis=0)
+        spec_buf[tm, :, tile * 128 : tile * 128 + 128] = both.astype(BF16)
+
+    own_spec = spec_buf.at[tm]
     for i in range(1, NTM):
-        x_copy(i).start()
+        remote(own_spec, own_spec, (x_sem.at[0], x_sem.at[1]), (lax.rem(tm + i, NTM), me)).start()
     inv_load.wait()
-    for i in range(1, NTM):
-        arrival(spec_buf, x_recv, lax.rem(tm + NTM - i, NTM)).wait()
-    spec = (spec_buf[0] + spec_buf[1]) + (spec_buf[2] + spec_buf[3])
+    landed(spec_buf.at[pl.ds(0, NTM - 1)], x_sem.at[1]).wait()
+    planes = [spec_buf[i].astype(F32) for i in range(NTM)]
+    spec = (planes[0] + planes[1]) + (planes[2] + planes[3])
     high = spec.astype(BF16)
     rest = (spec - high.astype(F32)).astype(BF16)
-    lags = dot(jnp.concatenate([high, rest], axis=0), inv_buf[...])
-    out_ref[...] = lags[0:8] + lags[8:16]
-
-    def sent(i, _):
-        d = lax.rem(me + i, NPAIR)
-        id_copy(d).wait_send()
-        main_copy(d).wait_send()
-        part_copy(d).wait_send()
-        return 0
-
-    lax.fori_loop(1, NPAIR, sent, 0)
-    for i in range(1, NTM):
-        x_copy(i).wait_send()
+    lags = dot(jnp.concatenate([high[0:8], rest[0:8]], axis=0), inv_buf[0:1024, :])
+    lags = lags + dot(jnp.concatenate([high[8:16], rest[8:16]], axis=0), inv_buf[1024:2048, :])
+    out_ref[...] = lags
+
+    landed(send_buf.at[pl.ds(0, NPAIR - 1)], send_sem).wait()
+    landed(id_buf.at[pl.ds(0, GROUP - 1)], id_sem.at[0]).wait()
+    landed(id_buf.at[pl.ds(0, NPAIR - GROUP)], id_sem.at[2]).wait()
+    landed(mid_buf.at[pl.ds(0, GROUP - 1)], part_sem.at[0]).wait()
+    landed(got_buf.at[:, pl.ds(0, GROUP - 1)], part_sem.at[2]).wait()
+    landed(spec_buf.at[pl.ds(0, NTM - 1)], x_sem.at[0]).wait()
 
 
 def on_device(strain, pair_list, pair_bins, bin_slots, seg_valid):
@@ -381,9 +388,9 @@
     smem = pl.BlockSpec(memory_space=pltpu.SMEM)
     hbm = pl.BlockSpec(memory_space=pl.ANY)
     dma = pltpu.SemaphoreType.DMA
-    return pl.pallas_call(
+    both = pl.pallas_call(
         body,
-        out_shape=jax.ShapeDtypeStruct((8, LAGS // NTM), F32),
+        out_shape=jax.ShapeDtypeStruct((16, LAGS // NTM), F32),
         in_specs=[hbm, hbm, hbm, vmem, vmem, smem, smem, smem],
         out_specs=vmem,
         scratch_shapes=[
@@ -403,11 +410,11 @@
             pltpu.VMEM((512, 4096), BF16),
             pltpu.VMEM((NPAIR * 128, 128), F32),
             pltpu.VMEM((4096, 256), BF16),
-            pltpu.VMEM((NPAIR, 2, 128), F32),
-            pltpu.VMEM((NPAIR, 2, 128), F32),
-            pltpu.VMEM((NTM, 8, 2 * BAND), F32),
-            dma((7,)), dma((NPAIR,)), dma((NPAIR,)), dma((NPAIR,)), dma((NPAIR,)),
-            dma((NPAIR,)), dma((NPAIR,)), dma((NTM,)), dma((NTM,)),
+            pltpu.VMEM((GROUP, GROUP, 2, 128), F32),
+            pltpu.VMEM((GROUP, GROUP, 2, 128), F32),
+            pltpu.VMEM((GROUP, GROUP, 2, 128), F32),
+            pltpu.VMEM((NTM, 16, BAND), BF16),
+            dma((7,)), dma, dma((NPAIR,)), dma((4,)), dma((4,)), dma((2,)),
         ],
         compiler_params=pltpu.CompilerParams(
             collective_id=0, has_side_effects=True, vmem_limit_bytes=60 << 20
@@ -422,6 +429,7 @@
         bin_slots,
         seg_valid,
     )
+    return both[0:8] + both[8:16]
 
 
 def solution(mesh):

time: 82.4 us -> 69.2 us (0.84)
  Pallas kernels: 80.9 us -> 67.6 us
  other arithmetic: 0 us -> 1.34 us
  local copies, waits for them, and re-layouts: 1.32 us -> 0 us
    pallas_call x1, Pallas kernels: 80.9 us -> 67.6 us  [on_device(): pl.pallas_call(body, out_shape=jax.ShapeDtypeStruct((16, LAGS // NTM), F3...]
    add x0 -> x1, other arithmetic: none -> 1.34 us  [on_device(): return both[0:8] + both[8:16]]
    unnamed x1 -> x0, local copies, waits for them, and re-layouts: 1.32 us -> none
where the time goes in v1:
time: 69.2 us; the launch traced here: 69 us
  Pallas kernels  67.6 us (98%)
  other arithmetic  1.34 us (2%)
    pallas_call x1, Pallas kernels, on_device(): pl.pallas_call(body, out_shape=jax.ShapeDtypeStruct((16, LAGS // NTM), F3...  67.6 us

profile of v1, /device:TPU:1, one launch (start us, length us, event | category | flops | bytes accessed | tf_op | source)
XLA Modules:
  0.0 69.0 jit_solution(18160849190954239382)
XLA Ops:
  0.0 67.6 %shard_map.82 = f32[16,512]{1,0:T(8,128)} custom-call(bf16[2,128,8192]{2,1,0:T(8,128)(2,1)} %x_hbm.1, bf16[4,512,2048]{2,1,0:T(8,128)(2,1)} %constant.6.clone.tab_hbm, bf16[4,2048,512]{2,1,0:T(8,128)(2,1)} %constant.7.clone.inv_hbm, bf16[1024,128]{1,0:T(8,128)(2,1)} %constant.8.clone.fold_ref, s32[2,4096]{1,0:T(2,128)} %bitcast.1, s32[64]{0:T(128)} %bins_smem.1, ...), custom_call_target="tpu_custom_call" | custom-call | tf_op jit(solution)/shard_map/pallas_call | solution.py:391
  67.6 1.3 %slice_add_fusion = f32[8,512]{1,0:T(8,128)} fusion(f32[16,512]{1,0:T(8,128)} %shard_map.82), kind=kLoop, calls=%fused_computation | loop fusion | flops 4096 | bytes 49152 | tf_op jit(solution)/shard_map/add | solution.py:432

commit v2 on v1

--- a/solution.py
+++ b/solution.py
@@ -16,6 +16,7 @@
 EPS = 1e-06
 NPAIR = 64
 NTM = 4
+STEP = 129
 GROUP = 8
 SUB = SEG_LEN // 8
 MESH = pl.DeviceIdType.MESH
@@ -91,7 +92,7 @@
     out_ref,
     x_buf, tab_buf, inv_buf, y_buf, r_buf, send_buf, recv_buf, id_buf,
     src_rows, loc_rows, loc_mat, g1_buf, g2_buf, s_buf, rows_buf, p_buf,
-    part_buf, mid_buf, got_buf, spec_buf,
+    part_buf, got_buf, spec_buf,
     load_sem, send_sem, recv_sem, id_sem, part_sem, x_sem,
 ):
     tm = lax.axis_index("tm")
@@ -200,8 +201,11 @@
     def landed(ref, sem):
         return pltpu.make_async_copy(ref, ref, sem)
 
-    def main_copy(i):
-        d = lax.rem(me + i, NPAIR)
+    def offset(n):
+        return (32 + n // 2 * (1 - n % 2 * 2)) * jnp.minimum(n, 1)
+
+    def main_copy(n):
+        d = lax.rem(me + offset(n), NPAIR)
         return remote(send_buf.at[d], recv_buf.at[me], (send_sem, recv_sem.at[me]), (tm, d))
 
     def send_main(i, _):
@@ -247,7 +251,7 @@
             earlier.append(jnp.where(hit, 1.0, 0.0).astype(BF16))
         slot_b = dot(jnp.concatenate(earlier, axis=0), ones_sq)
         for j in range(asks):
-            code = 2.0 * cols[j] + slot_b[j * 128 : j * 128 + 128]
+            code = cols[j] + 64.0 * slot_b[j * 128 : j * 128 + 128]
             g2 = jnp.where(code == lane_f, 1.0, 0.0).astype(BF16)
             g2_buf[base + j] = g2
             loc = jnp.broadcast_to(loc_rows[pl.ds(base + j, 1), :], (16, 128)).astype(BF16)
@@ -259,7 +263,7 @@
     loc_cols = loc_mat[...].astype(BF16)
 
     def choose(s, _):
-        pick = iota((128, 256), 0) == 2 * s + iota((128, 256), 1) // 128
+        pick = iota((128, 256), 0) == s + iota((128, 256), 1) // 128 * 64
         loc_b = dot(loc_cols, pick.astype(BF16))
         loc_b = 2.0 * jnp.concatenate([loc_b[:, 0:128], loc_b[:, 128:256]], axis=0)
         g1_buf[s, :, 0:128] = jnp.where(loc_b == lane_f, 1.0, 0.0).astype(BF16)
@@ -280,7 +284,7 @@
 
     def take(step, _):
         first = step * batch
-        sources = [lax.rem(me + NPAIR - first - j, NPAIR) for j in range(batch)]
+        sources = [lax.rem(me + NPAIR - offset(first + j), NPAIR) for j in range(batch)]
         for j, s in enumerate(sources):
             if j == 0:
 
@@ -299,7 +303,7 @@
                         piece = recv_buf[s, at : at + 16, :]
                         halves = [piece, zero] if ch == 0 else [zero, piece]
                         rows.append(jnp.concatenate(halves, axis=1))
-            rows_buf[pl.ds(pl.multiple_of(s * 128, 128), 128), :] = dot_nt(
+            rows_buf[pl.ds(s * STEP, 128), :] = dot_nt(
                 g1_buf[s], jnp.concatenate(rows, axis=0)
             )
         return 0
@@ -307,7 +311,8 @@
     lax.fori_loop(0, NPAIR // batch, take, 0)
 
     def cross(p, _):
-        asked = rows_buf[pl.ds(p, 128, stride=64), :].astype(BF16)
+        asked = [rows_buf[pl.ds(p + 64 * j, 64, stride=STEP), :] for j in range(2)]
+        asked = jnp.concatenate(asked, axis=0).astype(BF16)
         sides = dot(g2_buf[p], asked)
         left, right = sides[0:64], sides[64:128]
         to = pl.ds(pl.multiple_of(p * 64, 64), 64)
@@ -319,34 +324,32 @@
 
     seg = (iota((1, 256), 1) >> 4) & 1
     weight = jnp.where(seg == 0, valid_smem[0], valid_smem[1]).astype(F32)
+    z = dot(s_buf[...], p_buf[...]) * weight
+    high = z.astype(BF16)
+    rest = (z - high.astype(F32)).astype(BF16)
     total = jnp.zeros((128, 128), F32)
     for q in range(4):
-        z = dot(s_buf[q * 128 : q * 128 + 128, :], p_buf[...]) * weight
-        high = z.astype(BF16)
-        rest = (z - high.astype(F32)).astype(BF16)
         fold = fold_ref[q * 256 : q * 256 + 256, :]
-        total = total + (dot(high, fold) + dot(rest, fold))
+        part = slice(q * 128, q * 128 + 128)
+        total = total + (dot(high[part], fold) + dot(rest[part], fold))
     for d in range(NPAIR):
-        part_buf[d // GROUP, d % GROUP] = total[2 * d : 2 * d + 2, :]
-
-    group = me // GROUP
-    for i in range(1, GROUP):
-        to = across(i)
-        remote(part_buf.at[to // GROUP], mid_buf.at[group], (part_sem.at[0], part_sem.at[1]), (tm, to)).start()
-    mid_buf[group] = part_buf[group]
-    landed(mid_buf.at[pl.ds(0, GROUP - 1)], part_sem.at[1]).wait()
-    for i in range(1, GROUP):
-        to = beside(i)
-        remote(mid_buf.at[:, lax.rem(to, GROUP)], got_buf.at[:, mine], (part_sem.at[2], part_sem.at[3]), (tm, to)).start()
-    got_buf[:, pl.ds(mine, 1)] = mid_buf[:, pl.ds(mine, 1)]
-    landed(got_buf.at[:, pl.ds(0, GROUP - 1)], part_sem.at[3]).wait()
+        part_buf[d] = total[2 * d : 2 * d + 2, :]
+
+    def send_part(n, _):
+        d = lax.rem(me + offset(n), NPAIR)
+        remote(part_buf.at[d], got_buf.at[me], (part_sem.at[0], part_sem.at[1]), (tm, d)).start()
+        return 0
+
+    lax.fori_loop(1, NPAIR, send_part, 0)
+    got_buf[me] = part_buf[me]
+    landed(got_buf.at[pl.ds(0, NPAIR - 1)], part_sem.at[1]).wait()
 
     sub8, lane8 = iota((8, 128), 0), iota((8, 128), 1)
     def spread(tile):
         made = jnp.zeros((8, 128), F32)
         for j in range(4):
             d = 4 * tile + j
-            two = got_buf[d // GROUP, d % GROUP]
+            two = got_buf[d]
             both = jnp.where(
                 sub8 < 4,
                 jnp.broadcast_to(two[0:1, :], (8, 128)),
@@ -378,8 +381,7 @@
     landed(send_buf.at[pl.ds(0, NPAIR - 1)], send_sem).wait()
     landed(id_buf.at[pl.ds(0, GROUP - 1)], id_sem.at[0]).wait()
     landed(id_buf.at[pl.ds(0, NPAIR - GROUP)], id_sem.at[2]).wait()
-    landed(mid_buf.at[pl.ds(0, GROUP - 1)], part_sem.at[0]).wait()
-    landed(got_buf.at[:, pl.ds(0, GROUP - 1)], part_sem.at[2]).wait()
+    landed(part_buf.at[pl.ds(0, NPAIR - 1)], part_sem.at[0]).wait()
     landed(spec_buf.at[pl.ds(0, NTM - 1)], x_sem.at[0]).wait()
 
 
@@ -408,13 +410,12 @@
             pltpu.VMEM((NPAIR, 128, 256), BF16),
             pltpu.VMEM((NPAIR, 128, 128), BF16),
             pltpu.VMEM((512, 4096), BF16),
-            pltpu.VMEM((NPAIR * 128, 128), F32),
+            pltpu.VMEM((NPAIR * STEP, 128), F32),
             pltpu.VMEM((4096, 256), BF16),
-            pltpu.VMEM((GROUP, GROUP, 2, 128), F32),
-            pltpu.VMEM((GROUP, GROUP, 2, 128), F32),
-            pltpu.VMEM((GROUP, GROUP, 2, 128), F32),
+            pltpu.VMEM((NPAIR, 2, 128), F32),
+            pltpu.VMEM((NPAIR, 2, 128), F32),
             pltpu.VMEM((NTM, 16, BAND), BF16),
-            dma((7,)), dma, dma((NPAIR,)), dma((4,)), dma((4,)), dma((2,)),
+            dma((7,)), dma, dma((NPAIR,)), dma((4,)), dma((2,)), dma((2,)),
         ],
         compiler_params=pltpu.CompilerParams(
             collective_id=0, has_side_effects=True, vmem_limit_bytes=60 << 20

time: 69.2 us -> 62.8 us (0.908)
  Pallas kernels: 67.6 us -> 61.3 us
    pallas_call x1, Pallas kernels: 67.6 us -> 61.3 us  [on_device(): pl.pallas_call(body, out_shape=jax.ShapeDtypeStruct((16, LAGS // NTM), F3...]
where the time goes in v2:
time: 62.8 us; the launch traced here: 62.7 us
  Pallas kernels  61.3 us (98%)
  other arithmetic  1.34 us (2%)
    pallas_call x1, Pallas kernels, on_device(): pl.pallas_call(body, out_shape=jax.ShapeDtypeStruct((16, LAGS // NTM), F3...  61.3 us
    add x1, other arithmetic, on_device(): return both[0:8] + both[8:16]  1.34 us

profile of v2, /device:TPU:1, one launch (start us, length us, event | category | flops | bytes accessed | tf_op | source)
XLA Modules:
  0.0 62.7 jit_solution(4769890621223342422)
XLA Ops:
  0.0 61.3 %shard_map.82 = f32[16,512]{1,0:T(8,128)} custom-call(bf16[2,128,8192]{2,1,0:T(8,128)(2,1)} %x_hbm.1, bf16[4,512,2048]{2,1,0:T(8,128)(2,1)} %constant.6.clone.tab_hbm, bf16[4,2048,512]{2,1,0:T(8,128)(2,1)} %constant.7.clone.inv_hbm, bf16[1024,128]{1,0:T(8,128)(2,1)} %constant.8.clone.fold_ref, s32[2,4096]{1,0:T(2,128)} %bitcast.1, s32[64]{0:T(128)} %bins_smem.1, ...), custom_call_target="tpu_custom_call" | custom-call | tf_op jit(solution)/shard_map/pallas_call | solution.py:393
  61.3 1.3 %slice_add_fusion = f32[8,512]{1,0:T(8,128)} fusion(f32[16,512]{1,0:T(8,128)} %shard_map.82), kind=kLoop, calls=%fused_computation | loop fusion | flops 4096 | bytes 49152 | tf_op jit(solution)/shard_map/add | solution.py:433

commit v3 on v2

--- a/solution.py
+++ b/solution.py
@@ -17,6 +17,7 @@
 NPAIR = 64
 NTM = 4
 STEP = 129
+ID_STEP = 32
 GROUP = 8
 SUB = SEG_LEN // 8
 MESH = pl.DeviceIdType.MESH
@@ -51,7 +52,9 @@
                 table[c, :, 0, a, :, 1] = sign[a] * sin[c, :, a]
                 table[c, :, 1, a, :, 0] = -sin[c, :, a]
                 table[c, :, 1, a, :, 1] = sign[a] * cos[c, :, a]
-    return table.reshape(4, 512, 2 * SUB).astype(jnp.bfloat16)
+    first = np.stack([table[0, :, :, a, :, a] for a in range(2)])
+    rest = table[1:].reshape(3, 512, 2 * SUB)
+    return first.reshape(512, SUB).astype(jnp.bfloat16), rest.astype(jnp.bfloat16)
 
 
 def inverse_tables():
@@ -88,9 +91,9 @@
 
 
 def body(
-    x_hbm, tab_hbm, inv_hbm, fold_ref, pairs_ref, bins_smem, slots_smem, valid_smem,
+    x_hbm, real_hbm, tab_hbm, inv_hbm, fold_hbm, pairs_hbm, bins_smem, slots_smem, valid_smem,
     out_ref,
-    x_buf, tab_buf, inv_buf, y_buf, r_buf, send_buf, recv_buf, id_buf,
+    x_buf, real_buf, tab_buf, inv_buf, fold_ref, pairs_ref, y_buf, r_buf, send_buf, recv_buf, id_buf,
     src_rows, loc_rows, loc_mat, g1_buf, g2_buf, s_buf, rows_buf, p_buf,
     part_buf, got_buf, spec_buf,
     load_sem, send_sem, recv_sem, id_sem, part_sem, x_sem,
@@ -98,26 +101,33 @@
     tm = lax.axis_index("tm")
     me = lax.axis_index("pair")
 
-    def x_load(s):
-        return pltpu.make_async_copy(x_hbm.at[s], x_buf.at[s], load_sem.at[s])
+    def x_load(n):
+        rows = pl.ds(n % 2 * 64, 64)
+        return pltpu.make_async_copy(x_hbm.at[n // 2, rows], x_buf.at[n // 2, rows], load_sem.at[n])
 
     def tab_load(c):
-        return pltpu.make_async_copy(tab_hbm.at[c], tab_buf.at[c], load_sem.at[2 + c])
-
-    inv_load = pltpu.make_async_copy(inv_hbm.at[tm], inv_buf, load_sem.at[6])
-    x_load(0).start()
-    x_load(1).start()
+        if c == 0:
+            return pltpu.make_async_copy(real_hbm, real_buf, load_sem.at[4])
+        return pltpu.make_async_copy(tab_hbm.at[c - 1], tab_buf.at[c - 1], load_sem.at[4 + c])
+
+    inv_load = pltpu.make_async_copy(inv_hbm.at[tm], inv_buf, load_sem.at[8])
+    fold_load = pltpu.make_async_copy(fold_hbm, fold_ref, load_sem.at[9])
+    pairs_load = pltpu.make_async_copy(pairs_hbm, pairs_ref, load_sem.at[10])
+    for n in range(4):
+        x_load(n).start()
     for c in range(4):
         tab_load(c).start()
+    pairs_load.start()
     inv_load.start()
+    fold_load.start()
 
     barrier = pltpu.get_barrier_semaphore()
 
-    def greet(i, _):
+    def greet(i):
         pl.semaphore_signal(barrier, inc=1, device_id=(tm, lax.rem(me + i, NPAIR)), device_id_type=MESH)
-        return 0
-
-    lax.fori_loop(1, NPAIR, greet, 0)
+
+    for i in range(1, 8):
+        greet(i)
     for i in range(1, NTM):
         pl.semaphore_signal(barrier, inc=1, device_id=(lax.rem(tm + i, NTM), me), device_id_type=MESH)
 
@@ -132,12 +142,16 @@
     id_buf[me] = lax.fori_loop(0, 64, one_id, jnp.zeros((1, 128), jnp.int32))
 
     root = math.sqrt(0.5)
-    for s in range(2):
-        x_load(s).wait()
-
-        def split(step, _):
-            rows = pl.ds(pl.multiple_of(step * 16, 16), 16)
-            to = pl.ds(pl.multiple_of(s * 128 + step * 16, 16), 16)
+    greeted = (8, 24, 40, 52)
+    for n in range(4):
+        x_load(n).wait()
+
+        def split(step, _, n=n):
+            s, some = n // 2, (4, 4, 3, 3)[n]
+            for j in range(some):
+                greet(greeted[n] + step * some + j)
+            rows = pl.ds(pl.multiple_of(n % 2 * 64 + step * 16, 16), 16)
+            to = pl.ds(pl.multiple_of(n * 64 + step * 16, 16), 16)
             for h in range(2):
                 v = [
                     x_buf[s, rows, e * SUB + h * 512 : e * SUB + h * 512 + 512].astype(F32)
@@ -159,38 +173,10 @@
                         y_buf[c, to, at : at + 512] = parts[c][part].astype(BF16)
             return 0
 
-        lax.fori_loop(0, 8, split, 0)
-
-    for c in range(4):
-        tab_load(c).wait()
-        r_buf[c] = dot_nt(tab_buf[c], y_buf[c])
-
-    def white(w, _):
-        rows = pl.ds(pl.multiple_of(w * 32, 32), 32)
-        parts = [r_buf[c, rows, :] for c in range(4)]
-        power = parts[0] * parts[0]
-        for c in range(1, 4):
-            power = power + parts[c] * parts[c]
-        energy = jnp.sum(power, axis=0, keepdims=True) * (1.0 / 64.0)
-        scale = 1.0 / jnp.sqrt(energy + EPS)
-        for c in range(4):
-            done = (parts[c] * scale).astype(BF16)
-            send_buf[c * 16 + w, 0:32, :] = done[:, 0:128]
-            send_buf[c * 16 + w, 32:64, :] = done[:, 128:256]
-        return 0
-
-    lax.fori_loop(0, 16, white, 0)
-
-    pl.semaphore_wait(barrier, NPAIR - 1 + NTM - 1)
+        lax.fori_loop(0, 4, split, 0)
 
     here = me // GROUP * GROUP
     mine = lax.rem(me, GROUP)
-
-    def beside(i):
-        return here + lax.rem(mine + i, GROUP)
-
-    def across(i):
-        return lax.rem(me + i * GROUP, NPAIR)
 
     def remote(src, dst, sems, to):
         return pltpu.make_async_remote_copy(
@@ -204,23 +190,55 @@
     def offset(n):
         return (32 + n // 2 * (1 - n % 2 * 2)) * jnp.minimum(n, 1)
 
-    def main_copy(n):
+    for c in range(4):
+        tab_load(c).wait()
+        if c == 0:
+            r_buf[0, 0:256] = dot_nt(real_buf[0:256], y_buf[0, :, 0:SUB])
+            r_buf[0, 256:512] = dot_nt(real_buf[256:512], y_buf[0, :, SUB : 2 * SUB])
+        else:
+            r_buf[c] = dot_nt(tab_buf[c - 1], y_buf[c])
+
+    def white(w):
+        rows = pl.ds(pl.multiple_of(w * 32, 32), 32)
+        both = [r_buf[0, pl.ds(pl.multiple_of(a * 256 + w * 16, 16), 16), :] for a in range(2)]
+        real = jnp.concatenate([both[0][0:8], both[1][0:8], both[0][8:16], both[1][8:16]], axis=0)
+        parts = [real] + [r_buf[c, rows, :] for c in range(1, 4)]
+        power = parts[0] * parts[0]
+        for c in range(1, 4):
+            power = power + parts[c] * parts[c]
+        energy = jnp.sum(power, axis=0, keepdims=True) * (1.0 / 64.0)
+        scale = lax.rsqrt(energy + EPS)
+        for c in range(4):
+            done = (parts[c] * scale).astype(BF16)
+            send_buf[c * 16 + w, 0:32, :] = done[:, 0:128]
+            send_buf[c * 16 + w, 32:64, :] = done[:, 128:256]
+
+    def white_step(w, _):
+        white(w)
+        return 0
+
+    lax.fori_loop(0, 16, white_step, 0, unroll=8)
+
+    pl.semaphore_wait(barrier, NPAIR - 1 + NTM - 1)
+
+    for i in range(1, GROUP):
+        to = here + lax.rem(mine + i, GROUP)
+        remote(id_buf.at[me], id_buf.at[me], (id_sem.at[0], id_sem.at[1]), (tm, to)).start()
+
+    def send_main(n, _):
         d = lax.rem(me + offset(n), NPAIR)
-        return remote(send_buf.at[d], recv_buf.at[me], (send_sem, recv_sem.at[me]), (tm, d))
-
-    def send_main(i, _):
-        main_copy(i).start()
-        return 0
-
-    for i in range(1, GROUP):
-        remote(id_buf.at[me], id_buf.at[me], (id_sem.at[0], id_sem.at[1]), (tm, beside(i))).start()
-    lax.fori_loop(1, 32, send_main, 0)
+        remote(send_buf.at[d], recv_buf.at[me], (send_sem, recv_sem.at[me]), (tm, d)).start()
+        return 0
+
+    lax.fori_loop(1, ID_STEP, send_main, 0)
     landed(id_buf.at[pl.ds(0, GROUP - 1)], id_sem.at[1]).wait()
     own_group = id_buf.at[pl.ds(here, GROUP)]
     for i in range(1, GROUP):
-        remote(own_group, own_group, (id_sem.at[2], id_sem.at[3]), (tm, across(i))).start()
-    lax.fori_loop(32, NPAIR, send_main, 0)
+        to = lax.rem(me + i * GROUP, NPAIR)
+        remote(own_group, own_group, (id_sem.at[2], id_sem.at[3]), (tm, to)).start()
+    lax.fori_loop(ID_STEP, NPAIR, send_main, 0)
     recv_buf[me] = send_buf[me]
+    pairs_load.wait()
 
     low = iota((1, 128), 1) < 64
     for q in range(32):
@@ -285,15 +303,13 @@
     def take(step, _):
         first = step * batch
         sources = [lax.rem(me + NPAIR - offset(first + j), NPAIR) for j in range(batch)]
-        for j, s in enumerate(sources):
-            if j == 0:
-
-                @pl.when(first > 0)
-                def _():
-                    landed(recv_buf.at[s], recv_sem.at[s]).wait()
-
-            else:
-                landed(recv_buf.at[s], recv_sem.at[s]).wait()
+
+        @pl.when(first > 0)
+        def _():
+            landed(recv_buf.at[sources[0]], recv_sem.at[sources[0]]).wait()
+
+        for s in sources[1:]:
+            landed(recv_buf.at[s], recv_sem.at[s]).wait()
         for s in sources:
             rows = []
             for ri in range(2):
@@ -308,7 +324,7 @@
             )
         return 0
 
-    lax.fori_loop(0, NPAIR // batch, take, 0)
+    lax.fori_loop(0, 16, take, 0)
 
     def cross(p, _):
         asked = [rows_buf[pl.ds(p + 64 * j, 64, stride=STEP), :] for j in range(2)]
@@ -324,6 +340,7 @@
 
     seg = (iota((1, 256), 1) >> 4) & 1
     weight = jnp.where(seg == 0, valid_smem[0], valid_smem[1]).astype(F32)
+    fold_load.wait()
     z = dot(s_buf[...], p_buf[...]) * weight
     high = z.astype(BF16)
     rest = (z - high.astype(F32)).astype(BF16)
@@ -393,12 +410,15 @@
     both = pl.pallas_call(
         body,
         out_shape=jax.ShapeDtypeStruct((16, LAGS // NTM), F32),
-        in_specs=[hbm, hbm, hbm, vmem, vmem, smem, smem, smem],
+        in_specs=[hbm, hbm, hbm, hbm, hbm, hbm, smem, smem, smem],
         out_specs=vmem,
         scratch_shapes=[
             pltpu.VMEM((2, 128, SEG_LEN), BF16),
-            pltpu.VMEM((4, 512, 2 * SUB), BF16),
+            pltpu.VMEM((512, SUB), BF16),
+            pltpu.VMEM((3, 512, 2 * SUB), BF16),
             pltpu.VMEM((2 * BAND, LAGS // NTM), BF16),
+            pltpu.VMEM((1024, 128), BF16),
+            pltpu.VMEM((2, 4096), jnp.int32),
             pltpu.VMEM((4, 256, 2 * SUB), BF16),
             pltpu.VMEM((4, 512, 256), F32),
             pltpu.VMEM((NPAIR, 64, 128), BF16),
@@ -415,14 +435,14 @@
             pltpu.VMEM((NPAIR, 2, 128), F32),
             pltpu.VMEM((NPAIR, 2, 128), F32),
             pltpu.VMEM((NTM, 16, BAND), BF16),
-            dma((7,)), dma, dma((NPAIR,)), dma((4,)), dma((2,)), dma((2,)),
+            dma((11,)), dma, dma((NPAIR,)), dma((4,)), dma((2,)), dma((2,)),
         ],
         compiler_params=pltpu.CompilerParams(
             collective_id=0, has_side_effects=True, vmem_limit_bytes=60 << 20
         ),
     )(
         strain,
-        jnp.asarray(forward_tables()),
+        *(jnp.asarray(table) for table in forward_tables()),
         jnp.asarray(inverse_tables()),
         jnp.asarray(fold_table()),
         pair_list.T,

time: 62.8 us -> 60.2 us (0.959)
  Pallas kernels: 61.3 us -> 58.6 us
    pallas_call x1, Pallas kernels: 61.3 us -> 58.6 us  [on_device(): pl.pallas_call(body, out_shape=jax.ShapeDtypeStruct((16, LAGS // NTM), F3...]
where the time goes in v3:
time: 60.2 us; the launch traced here: 60 us
  Pallas kernels  58.6 us (97%)
  other arithmetic  1.34 us (2%)
    pallas_call x1, Pallas kernels, on_device(): pl.pallas_call(body, out_shape=jax.ShapeDtypeStruct((16, LAGS // NTM), F3...  58.6 us
    add x1, other arithmetic, on_device(): return both[0:8] + both[8:16]  1.34 us

profile of v3, /device:TPU:1, one launch (start us, length us, event | category | flops | bytes accessed | tf_op | source)
XLA Modules:
  0.0 60.0 jit_solution(10777733197234921662)
XLA Ops:
  0.0 58.6 %shard_map.91 = f32[16,512]{1,0:T(8,128)} custom-call(bf16[2,128,8192]{2,1,0:T(8,128)(2,1)} %x_hbm.1, bf16[512,1024]{1,0:T(8,128)(2,1)} %constant.8.clone.real_hbm, bf16[3,512,2048]{2,1,0:T(8,128)(2,1)} %constant.9.clone.tab_hbm, bf16[4,2048,512]{2,1,0:T(8,128)(2,1)} %constant.10.clone.inv_hbm, bf16[1024,128]{1,0:T(8,128)(2,1)} %constant.11.clone.fold_hbm, ...), custom_call_target="tpu_custom_call" | custom-call | tf_op jit(solution)/shard_map/pallas_call | solution.py:410
  58.6 1.3 %slice_add_fusion = f32[8,512]{1,0:T(8,128)} fusion(f32[16,512]{1,0:T(8,128)} %shard_map.91), kind=kLoop, calls=%fused_computation | loop fusion | flops 4096 | bytes 49152 | tf_op jit(solution)/shard_map/add | solution.py:453

commit v4 on v3

--- a/solution.py
+++ b/solution.py
@@ -17,7 +17,7 @@
 NPAIR = 64
 NTM = 4
 STEP = 129
-ID_STEP = 32
+ID_STEP = 16
 GROUP = 8
 SUB = SEG_LEN // 8
 MESH = pl.DeviceIdType.MESH
@@ -298,7 +298,7 @@
 
     zero = jnp.zeros((16, 128), BF16)
 
-    batch = 4
+    batch = 8
 
     def take(step, _):
         first = step * batch
@@ -324,7 +324,7 @@
             )
         return 0
 
-    lax.fori_loop(0, 16, take, 0)
+    lax.fori_loop(0, NPAIR // batch, take, 0)
 
     def cross(p, _):
         asked = [rows_buf[pl.ds(p + 64 * j, 64, stride=STEP), :] for j in range(2)]
@@ -336,7 +336,7 @@
         p_buf[to, 128:256] = (left * pltpu.roll(right, 64, 1)).astype(BF16)
         return 0
 
-    lax.fori_loop(0, NPAIR, cross, 0, unroll=8)
+    lax.fori_loop(0, NPAIR, cross, 0, unroll=16)
 
     seg = (iota((1, 256), 1) >> 4) & 1
     weight = jnp.where(seg == 0, valid_smem[0], valid_smem[1]).astype(F32)

time: 60.2 us -> 58.7 us (0.975)
  Pallas kernels: 58.6 us -> 57.2 us
    pallas_call x1, Pallas kernels: 58.6 us -> 57.2 us  [on_device(): pl.pallas_call(body, out_shape=jax.ShapeDtypeStruct((16, LAGS // NTM), F3...]
where the time goes in v4:
time: 58.7 us; the launch traced here: 58.5 us
  Pallas kernels  57.2 us (97%)
  other arithmetic  1.34 us (2%)
    pallas_call x1, Pallas kernels, on_device(): pl.pallas_call(body, out_shape=jax.ShapeDtypeStruct((16, LAGS // NTM), F3...  57.2 us
    add x1, other arithmetic, on_device(): return both[0:8] + both[8:16]  1.34 us

profile of v4, /device:TPU:1, one launch (start us, length us, event | category | flops | bytes accessed | tf_op | source)
XLA Modules:
  0.0 58.5 jit_solution(8890558752033542194)
XLA Ops:
  0.0 57.2 %shard_map.91 = f32[16,512]{1,0:T(8,128)} custom-call(bf16[2,128,8192]{2,1,0:T(8,128)(2,1)} %x_hbm.1, bf16[512,1024]{1,0:T(8,128)(2,1)} %constant.8.clone.real_hbm, bf16[3,512,2048]{2,1,0:T(8,128)(2,1)} %constant.9.clone.tab_hbm, bf16[4,2048,512]{2,1,0:T(8,128)(2,1)} %constant.10.clone.inv_hbm, bf16[1024,128]{1,0:T(8,128)(2,1)} %constant.11.clone.fold_hbm, ...), custom_call_target="tpu_custom_call" | custom-call | tf_op jit(solution)/shard_map/pallas_call | solution.py:410
  57.2 1.3 %slice_add_fusion = f32[8,512]{1,0:T(8,128)} fusion(f32[16,512]{1,0:T(8,128)} %shard_map.91), kind=kLoop, calls=%fused_computation | loop fusion | flops 4096 | bytes 49152 | tf_op jit(solution)/shard_map/add | solution.py:453

commit v5 on v4

--- a/solution.py
+++ b/solution.py
@@ -217,7 +217,7 @@
         white(w)
         return 0
 
-    lax.fori_loop(0, 16, white_step, 0, unroll=8)
+    lax.fori_loop(0, 16, white_step, 0, unroll=16)
 
     pl.semaphore_wait(barrier, NPAIR - 1 + NTM - 1)
 
@@ -288,7 +288,7 @@
         g1_buf[s, :, 128:256] = jnp.where(loc_b + 1.0 == lane_f, 1.0, 0.0).astype(BF16)
         return 0
 
-    lax.fori_loop(0, NPAIR, choose, 0, unroll=4)
+    lax.fori_loop(0, NPAIR, choose, 0, unroll=8)
 
     landed(id_buf.at[pl.ds(0, NPAIR - GROUP)], id_sem.at[3]).wait()
     for q in range(32):

time: 58.7 us -> 58.5 us (level)
  no operation moved by 1% of the time
where the time goes in v5:
time: 58.5 us; the launch traced here: 58.3 us
  Pallas kernels  57 us (97%)
  other arithmetic  1.34 us (2%)
    pallas_call x1, Pallas kernels, on_device(): pl.pallas_call(body, out_shape=jax.ShapeDtypeStruct((16, LAGS // NTM), F3...  57 us
    add x1, other arithmetic, on_device(): return both[0:8] + both[8:16]  1.34 us

profile of v5, /device:TPU:1, one launch (start us, length us, event | category | flops | bytes accessed | tf_op | source)
XLA Modules:
  0.0 58.3 jit_solution(11801101775045162659)
XLA Ops:
  0.0 57.0 %shard_map.91 = f32[16,512]{1,0:T(8,128)} custom-call(bf16[2,128,8192]{2,1,0:T(8,128)(2,1)} %x_hbm.1, bf16[512,1024]{1,0:T(8,128)(2,1)} %constant.8.clone.real_hbm, bf16[3,512,2048]{2,1,0:T(8,128)(2,1)} %constant.9.clone.tab_hbm, bf16[4,2048,512]{2,1,0:T(8,128)(2,1)} %constant.10.clone.inv_hbm, bf16[1024,128]{1,0:T(8,128)(2,1)} %constant.11.clone.fold_hbm, ...), custom_call_target="tpu_custom_call" | custom-call | tf_op jit(solution)/shard_map/pallas_call | solution.py:410
  57.0 1.3 %slice_add_fusion = f32[8,512]{1,0:T(8,128)} fusion(f32[16,512]{1,0:T(8,128)} %shard_map.91), kind=kLoop, calls=%fused_computation | loop fusion | flops 4096 | bytes 49152 | tf_op jit(solution)/shard_map/add | solution.py:453
